TPU v7x, 32 devices: a whole 2x2x4 slice. The times are simulated.
32 devices in a mesh: group: 4 (over z), owner: 8 (over y, x, core).
Axes of the slice: x: 2, y: 2, z: 4, core: 2. Of those that a mesh axis runs over, the one named last changes fastest.
Arguments:
- port_rows: bfloat16 [16384, 1024], P(('group', 'owner')), may hold values from -6 to 6
- defect_owner: int32 [16384, 1], P(('group', 'owner')), may hold values from 0 to 7; in each aligned block of 512 rows (0 to 511, 512 to 1023, ...) at most 128 rows name the same one
- defect_half: int32 [16384], P(('group', 'owner')), may hold values from 0 to 1
- defect_port: int32 [16384], P(('group', 'owner')), may hold values from 0 to 1023
- subcircuit_maps: bfloat16 [64, 1024, 1024], P(('group', 'owner')), may hold values from -0.1875 to 0.1875
- schur_off: bfloat16 [4096, 1024], P(('group', 'owner')), may hold values from -0.1875 to 0.1875
- schur_diag: float32 [4096], P(('group', 'owner')), may hold values from 1 to 4
- pivot_order: int32 [2, 1024], replicated, may hold values from 0 to 1023, each once within a row
Outputs:
- panel: float32 [16384, 1024], P(('group', 'owner'))
Inputs may be any that keep to these rules, and one draw needn't show every extreme that they name: `defect_owner`: within the rows of one device, no owner is named by more than 128 defects, a bound that some block reaches. `pivot_order`: each row is a permutation of the ports.
All inputs are finite; a program needn't handle non-finite values.
Results may differ from a plain program's by a relative error of at most 0.012.
Values may be sent and summed in bfloat16 or wider, within the bound.
A program may use at most 128 MiB of HBM per device.

v0:
```python
import jax
import jax.numpy as jnp
from jax import lax
from jax.sharding import PartitionSpec as P


def swapped(shard, axis, stride):
    return lax.ppermute(shard, axis, [(i, i ^ 1 << stride) for i in range(lax.axis_size(axis))])


def slot_routes(keys, key_count, capacity, own_rows):
    matches = (keys[:, None] == jnp.arange(key_count, dtype=jnp.int32)[None, :]).astype(jnp.int32)
    before = jnp.cumsum(matches, axis=0) - matches
    slot_rank = jnp.sum(before * matches, axis=1)
    target = keys * capacity + slot_rank
    return (
        lax.broadcasted_iota(jnp.int32, (key_count * capacity, own_rows), 0) == target[None, :]
    ).astype(jnp.bfloat16)


def body(
    port_rows,
    defect_owner,
    defect_half,
    defect_port,
    subcircuit_maps,
    schur_off,
    schur_diag,
    pivot_order,
):
    own_rows, port_width = port_rows.shape
    owner_count = lax.axis_size("owner")
    sub_count = subcircuit_maps.shape[0]
    all_subs = owner_count * sub_count
    capacity = max(2, 2 * own_rows // owner_count)
    owner_ids = defect_owner[:, 0]
    columns = lax.broadcasted_iota(jnp.int32, (own_rows, port_width), 1)
    stimulus = (
        port_rows.astype(jnp.float32) + jnp.where(columns == defect_port[:, None], 8.0, 0.0)
    ).astype(jnp.bfloat16)
    sub_ids = owner_ids * sub_count + defect_half
    route_table = slot_routes(sub_ids, all_subs, capacity, own_rows)
    outgoing = jnp.dot(route_table, stimulus, preferred_element_type=jnp.float32).astype(
        jnp.bfloat16
    )
    outgoing = outgoing.reshape(owner_count, sub_count, capacity, port_width)
    answer = jnp.einsum(
        "oskp,spq->oskq",
        lax.all_to_all(outgoing, "owner", split_axis=0, concat_axis=0, tiled=True),
        subcircuit_maps,
        preferred_element_type=jnp.float32,
    ).astype(jnp.bfloat16)
    returned = lax.all_to_all(answer, "owner", split_axis=0, concat_axis=0, tiled=True)
    returned = returned.reshape(all_subs * capacity, port_width)
    response = lax.dot_general(
        route_table, returned, (((0,), (0,)), ((), ())), preferred_element_type=jnp.float32
    )
    first_diag = lax.all_gather(schur_diag, "owner", axis=0, tiled=True)
    level_count = lax.axis_size("group").bit_length() - 1
    assembled = []
    off_rows = schur_off.astype(jnp.float32)
    diag_rows = schur_diag
    for level in range(level_count):
        sibling_off, sibling_diag = (
            swapped(off_rows.astype(jnp.bfloat16), "group", level).astype(off_rows.dtype),
            swapped(diag_rows.astype(jnp.bfloat16), "group", level).astype(diag_rows.dtype),
        )
        off_rows = off_rows + jnp.take(sibling_off, pivot_order[level], axis=1)
        diag_rows = diag_rows + sibling_diag
        assembled.append(
            (
                lax.all_gather(off_rows.astype(jnp.bfloat16), "owner", axis=0, tiled=True),
                lax.all_gather(diag_rows.astype(jnp.bfloat16), "owner", axis=0, tiled=True).astype(
                    diag_rows.dtype
                ),
            )
        )
    panel = response / first_diag[None, :]
    for full_off, full_diag in assembled:
        coupled = lax.dot_general(
            panel.astype(jnp.bfloat16),
            full_off,
            (((1,), (1,)), ((), ())),
            preferred_element_type=jnp.float32,
        )
        panel = (response - coupled) / full_diag[None, :]
    return panel


def solution(mesh):
    return jax.shard_map(
        body,
        mesh=mesh,
        in_specs=(
            P(("group", "owner"), None),
            P(("group", "owner"), None),
            P(("group", "owner")),
            P(("group", "owner")),
            P(("group", "owner"), None, None),
            P(("group", "owner"), None),
            P(("group", "owner")),
            P(),
        ),
        out_specs=P(("group", "owner"), None),
        check_vma=False,
    )
```

profile of v0, /device:TPU:1, one launch (start us, length us, event | category | flops | bytes accessed | tf_op | source)
XLA Modules:
  0.0 188.0 jit_solution(8197324033343823637)
XLA Ops:
  6.5 0.7 broadcast_multiply_fusion
  7.2 0.7 add.27
  7.9 1.1 reduce-window.6
  9.1 0.2 slice_reduce_fusion
  9.3 0.1 fusion.20
  9.4 5.8 %fusion.5 = bf16[2048,1024]{1,0:T(8,128)(2,1)} fusion(s32[512]{0:T(512)S(1)} %multiply_add_fusion, bf16[512,1024]{1,0:T(8,128)(2,1)} %param.10, s32[512]{0:T(512)} %param.13), kind=kOutput, calls=%fused_computation.9 | convolution fusion | flops 2153250816 | bytes 5246976 | tf_op jit(solution)/shard_map/dot_general | solution.py:43
  15.2 0.0 copy-start
  15.2 0.0 copy-start.1
  15.2 5.4 %all-to-all-start = ((bf16[8,2,128,1024]{3,2,1,0:T(8,128)(2,1)}), bf16[8,2,128,1024]{3,2,1,0:T(8,128)(2,1)}, u32[]{:S(2)}, u32[]{:S(2)}) async-start(bf16[8,2,128,1024]{3,2,1,0:T(8,128)(2,1)} %bitcast.54), calls=%async_computation | async-start | bytes 8388608 | tf_op jit(solution)/shard_map/all_to_all | solution.py:49
  20.6 0.0 all-gather.6.cloned.1.call-start
  20.6 0.0 copy-done
  20.6 0.2 copy.20
  20.8 2.1 %collective-permute-start = (bf16[128,1024]{0,1:T(8,128)(2,1)S(1)}, bf16[128,1024]{0,1:T(8,128)(2,1)S(1)}, u32[]{:S(2)}, u32[]{:S(2)}) collective-permute-start(bf16[128,1024]{0,1:T(8,128)(2,1)S(1)} %copy.20), channel_id=1, source_target_pairs={{0,8},{8,0},{16,24},{24,16},{1,9},{9,1},{17,25},{25,17},{2,10},{10... | collective-permute-start | bytes 786440 | tf_op jit(solution)/shard_map/ppermute | solution.py:8
  22.8 0.0 copy-done.1
  22.9 6.7 %collective-permute-done = bf16[128,1024]{0,1:T(8,128)(2,1)S(1)} collective-permute-done((bf16[128,1024]{0,1:T(8,128)(2,1)S(1)}, bf16[128,1024]{0,1:T(8,128)(2,1)S(1)}, u32[]{:S(2)}, u32[]{:S(2)}) %collective-permute-start) | collective-permute-done | bytes 262176 | tf_op jit(solution)/shard_map/ppermute | solution.py:8
  29.6 2.8 %gather_fusion = f32[1024,128]{1,0:T(8,128)S(1)} fusion(f32[128,1024]{0,1:T(8,128)S(1)} %convert_element_type.77, s32[1024]{0:T(1024)S(1)} %fusion.22), kind=kCustom, calls=%fused_computation.clone | custom fusion | bytes 1052672 | tf_op jit(solution)/shard_map/jit(_take)/gather | solution.py:68
  32.4 0.9 fusion.17
  33.3 0.0 all-gather.6.cloned.1.call-update
  33.3 2.2 %collective-permute-start.2 = (bf16[128,1024]{0,1:T(8,128)(2,1)}, bf16[128,1024]{0,1:T(8,128)(2,1)S(1)}, u32[]{:S(2)}, u32[]{:S(2)}) collective-permute-start(bf16[128,1024]{0,1:T(8,128)(2,1)} %fusion.17), channel_id=1, source_target_pairs={{0,16},{8,24},{16,0},{24,8},{1,17},{9,25},{17,1},{25,9},{2,18},{10... | collective-permute-start | bytes 786440 | tf_op jit(solution)/shard_map/ppermute | solution.py:8
  35.6 34.4 %all-to-all-done = bf16[8,2,128,1024]{3,2,1,0:T(8,128)(2,1)} async-done(((bf16[8,2,128,1024]{3,2,1,0:T(8,128)(2,1)}), bf16[8,2,128,1024]{3,2,1,0:T(8,128)(2,1)}, u32[]{:S(2)}, u32[]{:S(2)}) %all-to-all-start) | async-done | bytes 4194336 | tf_op jit(solution)/shard_map/all_to_all | solution.py:49
  70.0 8.0 %convert_bitcast_fusion = bf16[8,2,128,1024]{3,2,0,1:T(8,128)(2,1)S(1)} fusion(bf16[2,1024,1024]{2,1,0:T(8,128)(2,1)} %param.14, bf16[8,2,128,1024]{3,2,1,0:T(8,128)(2,1)} %all-to-all-done), kind=kOutput, calls=%fused_computation.5 | convolution fusion | flops 4297064448 | bytes 12582912 | tf_op jit(solution)/shard_map/oskp,spq->oskq/dot_general | solution.py:47
  77.9 2.7 %copy.19 = bf16[8,2,128,1024]{3,2,1,0:T(8,128)(2,1)} copy(bf16[8,2,128,1024]{3,2,0,1:T(8,128)(2,1)S(1)} %convert_bitcast_fusion) | data formatting | bytes 8388608 | tf_op jit(solution)/shard_map/convert_element_type | solution.py:52
  80.6 8.9 %all-to-all-start.1 = ((bf16[8,2,128,1024]{3,2,1,0:T(8,128)(2,1)}), bf16[8,2,128,1024]{3,2,1,0:T(8,128)(2,1)}, u32[]{:S(2)}, u32[]{:S(2)}) async-start(bf16[8,2,128,1024]{3,2,1,0:T(8,128)(2,1)} %copy.19), calls=%async_computation.1 | async-start | bytes 8388608 | tf_op jit(solution)/shard_map/all_to_all | solution.py:53
  89.6 0.0 all-gather.8.cloned.1.call-start
  89.6 0.0 collective-permute-done.2
  89.6 0.0 copy-start.2
  89.7 2.8 %gather_fusion.1 = f32[1024,128]{1,0:T(8,128)S(1)} fusion(f32[128,1024]{0,1:T(8,128)S(1)} %convert_element_type.84, s32[1024]{0:T(1024)S(1)} %fusion.23), kind=kCustom, calls=%fused_computation.1.clone | custom fusion | bytes 1052672 | tf_op jit(solution)/shard_map/jit(_take)/gather | solution.py:68
  92.5 1.1 fusion.16
  93.5 0.0 all-gather.8.cloned.1.call-update
  93.6 0.0 copy-done.2
  93.6 2.7 %collective-permute-start.1 = (bf16[128]{0:T(256)(128)(2,1)S(1)}, bf16[128]{0:T(256)(128)(2,1)S(1)}, u32[]{:S(2)}, u32[]{:S(2)}) collective-permute-start(bf16[128]{0:T(256)(128)(2,1)S(1)} %convert_element_type.79), channel_id=1, source_target_pairs={{0,8},{8,0},{16,24},{24,16},{1,9},{9,1},{17,25},{25,17},{2,10},{10... | collective-permute-start | bytes 776 | tf_op jit(solution)/shard_map/ppermute | solution.py:8
  96.2 53.7 %all-gather = f32[8,1,128]{2,1,0:T(1,128)S(1)} all-gather(f32[1,1,128]{2,1,0:T(1,128)S(1)} %bitcast.64), channel_id=1, replica_groups=mesh['group'=4,'owner'=8] {'owner'}, dimensions={0}, use_global_device_ids=true | all-gather | bytes 4608 | tf_op jit(solution)/shard_map/all_gather | solution.py:58
  149.9 0.0 collective-permute-done.1
  149.9 3.8 %collective-permute-start.3 = (bf16[128]{0:T(256)(128)(2,1)S(1)}, bf16[128]{0:T(256)(128)(2,1)S(1)}, u32[]{:S(2)}, u32[]{:S(2)}) collective-permute-start(bf16[128]{0:T(256)(128)(2,1)S(1)} %fusion.24), channel_id=1, source_target_pairs={{0,16},{8,24},{16,0},{24,8},{1,17},{9,25},{17,1},{25,9},{2,18},{10... | collective-permute-start | bytes 776 | tf_op jit(solution)/shard_map/ppermute | solution.py:8
  153.7 8.1 %all-gather.1 = bf16[8,1,128]{2,1,0:T(2,128)(2,1)S(1)} all-gather(bf16[1,1,128]{2,1,0:T(2,128)(2,1)S(1)} %bitcast.65), channel_id=1, replica_groups=mesh['group'=4,'owner'=8] {'owner'}, dimensions={0}, use_global_device_ids=true | all-gather | bytes 2304 | tf_op jit(solution)/shard_map/all_gather | solution.py:73
  161.8 0.0 collective-permute-done.3
  161.8 8.8 %all-gather.2 = bf16[8,1,128]{2,1,0:T(2,128)(2,1)S(1)} all-gather(bf16[1,1,128]{2,1,0:T(2,128)(2,1)S(1)} %convert_bitcast_fusion.1), channel_id=1, replica_groups=mesh['group'=4,'owner'=8] {'owner'}, dimensions={0}, use_global_device_ids=true | all-gather | bytes 2304 | tf_op jit(solution)/shard_map/all_gather | solution.py:73
  170.6 0.0 all-to-all-done.1
  170.6 4.6 %fusion.3 = f32[512,1024]{1,0:T(8,128)S(1)} fusion(bf16[2048,1024]{1,0:T(8,128)(2,1)} %bitcast.7, s32[512]{0:T(512)S(1)} %multiply_add_fusion), kind=kOutput, calls=%fused_computation.7 | convolution fusion | flops 2148532224 | bytes 6293504 | tf_op jit(solution)/shard_map/dot_general | solution.py:55
  175.2 0.0 all-gather.6.cloned.1.call-done
  175.2 0.0 all-gather.8.cloned.1.call-done
  175.3 5.9 %subtract_divide_fusion = f32[512,1024]{1,0:T(8,128)} fusion(f32[512,1024]{1,0:T(8,128)S(1)} %fusion.3, bf16[1024,1024]{0,1:T(8,128)(2,1)} %all-gather.8.cloned.1.call-done, f32[1024]{0:T(1024)S(1)} %bitcast.63, bf16[1024,1024]{0,1:T(8,128)(2,1)} %all-gather.6.cloned.1.call-done, f32[1024]{0:T(1024)S(1)} %bitcast.62, f32[1024]{0:T(1024)S(1)} %bitcast.61), kind=kOutput, calls=%fused_computation.10 | convolution fusion | flops 2151153664 | bytes 8400896 | tf_op jit(solution)/shard_map/dot_general | solution.py:80
  (16 shorter events, 0.2 us)
Async XLA Ops:
  15.2 5.4 %copy-start = (bf16[128,1024]{1,0:T(8,128)(2,1)S(1)}, bf16[128,1024]{1,0:T(8,128)(2,1)}, u32[]{:S(2)}) copy-start(bf16[128,1024]{1,0:T(8,128)(2,1)} %param.15) | copy-start | bytes 786436
  15.2 7.6 %copy-start.1 = (s32[2,1024]{1,0:T(2,128)S(1)}, s32[2,1024]{1,0:T(2,128)}, u32[]{:S(2)}) copy-start(s32[2,1024]{1,0:T(2,128)} %param.17) | copy-start | bytes 24580
  15.2 54.7 %all-to-all-start = ((bf16[8,2,128,1024]{3,2,1,0:T(8,128)(2,1)}), bf16[8,2,128,1024]{3,2,1,0:T(8,128)(2,1)}, u32[]{:S(2)}, u32[]{:S(2)}) async-start(bf16[8,2,128,1024]{3,2,1,0:T(8,128)(2,1)} %bitcast.54), calls=%async_computation | async-start | bytes 8388608 | tf_op jit(solution)/shard_map/all_to_all | solution.py:49
  20.6 154.6 %all-gather.6.cloned.1.call-start = ((), (), s32[]{:S(2)}) async-start(), calls=%async_computation.2 | async-start | bytes 2359296 | tf_op jit(solution)/shard_map/all_gather | solution.py:72
  20.8 8.8 %collective-permute-start = (bf16[128,1024]{0,1:T(8,128)(2,1)S(1)}, bf16[128,1024]{0,1:T(8,128)(2,1)S(1)}, u32[]{:S(2)}, u32[]{:S(2)}) collective-permute-start(bf16[128,1024]{0,1:T(8,128)(2,1)S(1)} %copy.20), channel_id=1, source_target_pairs={{0,8},{8,0},{16,24},{24,16},{1,9},{9,1},{17,25},{25,17},{2,10},{10... | collective-permute-start | bytes 786440 | tf_op jit(solution)/shard_map/ppermute | solution.py:8
  33.3 56.2 %collective-permute-start.2 = (bf16[128,1024]{0,1:T(8,128)(2,1)}, bf16[128,1024]{0,1:T(8,128)(2,1)S(1)}, u32[]{:S(2)}, u32[]{:S(2)}) collective-permute-start(bf16[128,1024]{0,1:T(8,128)(2,1)} %fusion.17), channel_id=1, source_target_pairs={{0,16},{8,24},{16,0},{24,8},{1,17},{9,25},{17,1},{25,9},{2,18},{10... | collective-permute-start | bytes 786440 | tf_op jit(solution)/shard_map/ppermute | solution.py:8
  80.6 90.0 %all-to-all-start.1 = ((bf16[8,2,128,1024]{3,2,1,0:T(8,128)(2,1)}), bf16[8,2,128,1024]{3,2,1,0:T(8,128)(2,1)}, u32[]{:S(2)}, u32[]{:S(2)}) async-start(bf16[8,2,128,1024]{3,2,1,0:T(8,128)(2,1)} %copy.19), calls=%async_computation.1 | async-start | bytes 8388608 | tf_op jit(solution)/shard_map/all_to_all | solution.py:53
  89.6 85.7 %all-gather.8.cloned.1.call-start = ((), (), s32[]{:S(2)}) async-start(), calls=%async_computation.3 | async-start | bytes 2359296 | tf_op jit(solution)/shard_map/all_gather | solution.py:72
  89.6 3.9 %copy-start.2 = (f32[128]{0:T(128)S(1)}, f32[128]{0:T(128)}, u32[]{:S(2)}) copy-start(f32[128]{0:T(128)} %param.16) | copy-start | bytes 1540
  93.6 56.4 %collective-permute-start.1 = (bf16[128]{0:T(256)(128)(2,1)S(1)}, bf16[128]{0:T(256)(128)(2,1)S(1)}, u32[]{:S(2)}, u32[]{:S(2)}) collective-permute-start(bf16[128]{0:T(256)(128)(2,1)S(1)} %convert_element_type.79), channel_id=1, source_target_pairs={{0,8},{8,0},{16,24},{24,16},{1,9},{9,1},{17,25},{25,17},{2,10},{10... | collective-permute-start | bytes 776 | tf_op jit(solution)/shard_map/ppermute | solution.py:8
  149.9 11.9 %collective-permute-start.3 = (bf16[128]{0:T(256)(128)(2,1)S(1)}, bf16[128]{0:T(256)(128)(2,1)S(1)}, u32[]{:S(2)}, u32[]{:S(2)}) collective-permute-start(bf16[128]{0:T(256)(128)(2,1)S(1)} %fusion.24), channel_id=1, source_target_pairs={{0,16},{8,24},{16,0},{24,8},{1,17},{9,25},{17,1},{25,9},{2,18},{10... | collective-permute-start | bytes 776 | tf_op jit(solution)/shard_map/ppermute | solution.py:8
Sparse Core Ops, SparseCore 0:
  33.5 46.3 all-gather.5
  93.7 50.2 all-gather.7
where the time goes:
time: 189 us; the launch traced here: 188 us
  blocking collectives  70.6 us (37%)
  waiting for transfers between devices  41.1 us (22%)
  starting transfers between devices  25 us (13%)
  matrix products  24.2 us (13%)
  between operations  13.6 us (7%)
  local copies, waits for them, and re-layouts  8.72 us (5%)
  other arithmetic  4.76 us (3%)
    all_gather x1, blocking collectives, body(): first_diag = lax.all_gather(schur_diag, 'owner', axis=0, tiled=True)  53.7 us
    all_to_all x1, waiting for transfers between devices, body(): lax.all_to_all(outgoing, 'owner', split_axis=0, concat_axis=0, tiled=True)  34.4 us
    all_gather x2, blocking collectives, body(): lax.all_gather(diag_rows.astype(jnp.bfloat16), 'owner', axis=0, tiled=True)  16.9 us
    ppermute x4, starting transfers between devices, swapped(): lax.ppermute(shard, axis, [(i, i ^ 1 << stride) for i in range(lax.axis_s...  10.7 us
    all_to_all x1, starting transfers between devices, body(): lax.all_to_all(answer, 'owner', split_axis=0, concat_axis=0, tiled=True)  8.95 us
    dot_general x1, matrix products, body(): jnp.einsum('oskp,spq->oskq', lax.all_to_all(outgoing, 'owner', split_axis...  7.96 us
    ppermute x4, waiting for transfers between devices, swapped(): lax.ppermute(shard, axis, [(i, i ^ 1 << stride) for i in range(lax.axis_s...  6.66 us
    dot_general x1, matrix products, body(): lax.dot_general(panel.astype(jnp.bfloat16), full_off, (((1,), (1,)), ((),...  5.89 us
  transfers between devices with their start and end apart: 8, of which 2 were waited for; matrix products, arithmetic and copies ran while one was open for 12% of the time, Pallas kernels for 0%

commit v1 on v0

v1 whole, which is shorter than its diff:
```python
import functools

import jax
import jax.numpy as jnp
from jax import lax
from jax.experimental import pallas as pl
from jax.experimental.pallas import tpu as pltpu
from jax.sharding import PartitionSpec as P

F32 = jnp.float32
BF16 = jnp.bfloat16
I32 = jnp.int32
MESH = pl.DeviceIdType.MESH
LANES = 128


def one_hot(mask):
    return jnp.where(mask, 1.0, 0.0).astype(BF16)


def kernel(
    n,
    levels,
    cap,
    rows_ref,
    owner_ref,
    half_ref,
    port_ref,
    maps_ref,
    off_ref,
    diag_ref,
    order_ref,
    out_ref,
    maps,
    stim,
    sent,
    got,
    answer,
    back,
    meta_sent,
    meta_got,
    blocks,
    current,
    swap,
    diag,
    diag_swap,
    diag_got,
    scale,
    target_col,
    response,
    panel,
    map_sem,
    sent_send,
    sent_recv,
    meta_send,
    meta_recv,
    back_send,
    back_recv,
    swap_send,
    swap_recv,
    dswap_send,
    dswap_recv,
    block_send,
    block_recv,
    twin_send,
    twin_recv,
    diag_send,
    diag_recv,
):
    own_rows, width = rows_ref.shape
    depth = off_ref.shape[0]
    chips = n // 2
    pair = 2 * cap
    me = lax.axis_index("owner")
    group = lax.axis_index("group")
    chip, core = lax.div(me, 2), lax.rem(me, 2)
    twin = chip * 2 + 1 - core
    started = []

    def partner(level):
        step = 1 << level
        return group + step * (1 - 2 * lax.rem(lax.div(group, step), 2))

    def remote(src, dst, send, recv, **where):
        return pltpu.make_async_remote_copy(
            src_ref=src,
            dst_ref=dst,
            send_sem=send,
            recv_sem=recv,
            device_id=where,
            device_id_type=MESH,
        )

    def start(copy):
        copy.start()
        started.append(copy)

    def span(at, size):
        return pl.ds(pl.multiple_of(at * size, size), size)

    def chip_to(i):
        return lax.rem(chip + i, chips)

    def chip_from(i):
        return lax.rem(chip + chips - i, chips)

    barrier = pltpu.get_barrier_semaphore()
    for i in range(1, n):
        pl.semaphore_signal(
            barrier, inc=1, device_id={"owner": lax.rem(me + i, n)}, device_id_type=MESH
        )
    for level in range(levels):
        pl.semaphore_signal(
            barrier, inc=1, device_id={"group": partner(level)}, device_id_type=MESH
        )

    load = pltpu.make_async_copy(maps_ref, maps, map_sem)
    load.start()

    owner_row, half_row = owner_ref[...], half_ref[...]
    sub_row = owner_row * 2 + half_row
    at_row = lax.broadcasted_iota(I32, (own_rows, own_rows), 0)
    at_col = lax.broadcasted_iota(I32, (own_rows, own_rows), 1)
    hit = lax.broadcasted_iota(I32, (2 * n, own_rows), 0) == sub_row
    before = jnp.dot(one_hot(hit), one_hot(at_row < at_col), preferred_element_type=F32)
    rank = jnp.sum(jnp.where(hit, before, 0.0), axis=0, keepdims=True)
    target_row = owner_row.astype(F32) * cap + jnp.where(half_row == 0, rank, cap - 1 - rank)
    target_col[...] = jnp.sum(
        jnp.where(at_row == at_col, target_row, 0.0), axis=1, keepdims=True
    )
    port_col = jnp.sum(
        jnp.where(at_row == at_col, port_ref[...].astype(F32), 0.0), axis=1, keepdims=True
    )
    response[:, :LANES] = jnp.broadcast_to(port_col, (own_rows, LANES))

    @pl.loop(0, own_rows // LANES)
    def _(t):
        tile = span(t, LANES)
        column = lax.broadcasted_iota(I32, (LANES, width), 1).astype(F32)
        injected = jnp.where(column == response[tile, :1], 8.0, 0.0)
        stim[tile, :] = (rows_ref[tile, :].astype(F32) + injected).astype(BF16)

    pl.semaphore_wait(barrier, n - 1 + levels)

    def start_swap(level):
        src = off_ref if level == 0 else blocks.at[level - 1, span(me, depth)]
        copy = remote(
            src, swap.at[level], swap_send.at[level], swap_recv.at[level], group=partner(level)
        )
        small = remote(
            diag.at[level],
            diag_swap.at[level],
            dswap_send.at[level],
            dswap_recv.at[level],
            group=partner(level),
        )
        start(copy)
        start(small)
        return copy, small

    diag[0] = diag_ref[...]
    swaps = start_swap(0)

    for i in [*range(1, chips), 0]:
        c = chip_to(i)
        slot = lax.broadcasted_iota(I32, (pair, own_rows), 0) + c * pair
        route = one_hot(slot.astype(F32) == target_row)
        sent[span(c, pair), :] = jnp.dot(
            route, stim[...], preferred_element_type=F32
        ).astype(BF16)
        for k in range(2):
            o = 2 * c + lax.rem(core + k, 2)
            first = jnp.sum(jnp.where(sub_row == 2 * o, 1.0, 0.0), axis=1, keepdims=True)
            if i == 0 and k == 0:
                got[span(me, cap), :] = sent[span(me, cap), :]
                meta_got[me] = jnp.broadcast_to(first, (8, LANES))
                continue
            at = 2 * i + k
            meta_sent[o] = jnp.broadcast_to(first, (8, LANES))
            start(
                remote(
                    sent.at[span(o, cap)],
                    got.at[span(me, cap)],
                    sent_send.at[at],
                    sent_recv.at[at],
                    owner=o,
                )
            )
            start(
                remote(
                    meta_sent.at[o], meta_got.at[me], meta_send.at[at], meta_recv.at[at], owner=o
                )
            )

    def assemble(level, pending):
        for copy in pending:
            copy.wait_recv()
        if level == 0:
            current[:depth, :] = off_ref[...].astype(F32)

        @pl.loop(0, width // 256)
        def _(t):
            tile = span(t, 256)
            order = order_ref[level : level + 1, tile]
            pick = one_hot(lax.broadcasted_iota(I32, (width, 256), 0) == order)
            total = current[:depth, tile] + jnp.dot(
                swap[level], pick, preferred_element_type=F32
            )
            current[:depth, tile] = total
            blocks[level, span(me, depth), tile] = total.astype(BF16)

        held = diag[level]
        total = held[level : level + 1] + diag_swap[level][level : level + 1]
        at = lax.broadcasted_iota(I32, held.shape, 0)
        diag[level + 1] = jnp.where(at == level + 1, total, held)
        nxt = start_swap(level + 1) if level + 1 < levels else ()
        own = blocks.at[level, span(me, depth)]
        for i in range(1, chips):
            start(
                remote(
                    own,
                    own,
                    block_send.at[level, i],
                    block_recv.at[level, i],
                    owner=2 * chip_to(i) + core,
                )
            )
        start(remote(own, own, twin_send.at[level, 0], twin_recv.at[level, 0], owner=twin))
        return nxt

    def answers(i):
        c = chip_from(i)
        for k in range(2):
            if i == 0 and k == 0:
                continue
            at = 2 * i + k
            o = 2 * c + lax.rem(core + k, 2)
            here = got.at[span(o, cap)]
            remote(here, here, sent_send.at[at], sent_recv.at[at], owner=o).wait_recv()
            tag = meta_got.at[o]
            remote(tag, tag, meta_send.at[at], meta_recv.at[at], owner=o).wait_recv()
        at = lax.broadcasted_iota(I32, (pair, 1), 0)
        even, odd = meta_got[2 * c], meta_got[2 * c + 1]
        limit = jnp.where(at < cap, even[:1, :1], odd[:1, :1] + cap)
        first = at.astype(F32) < limit

        @pl.loop(0, width // 256)
        def _(t):
            tile = span(t, 256)
            block = got[span(c, pair), :]
            zero = jnp.dot(block, maps[0, :, tile], preferred_element_type=F32)
            one = jnp.dot(block, maps[1, :, tile], preferred_element_type=F32)
            answer[span(c, pair), tile] = jnp.where(first, zero, one).astype(BF16)

        for k in range(2):
            at = 2 * i + k
            o = 2 * c + lax.rem(core + k, 2)
            if i == 0 and k == 0:
                back[span(me, cap), :] = answer[span(me, cap), :]
                continue
            start(
                remote(
                    answer.at[span(o, cap)],
                    back.at[span(me, cap)],
                    back_send.at[at],
                    back_recv.at[at],
                    owner=o,
                )
            )

    swaps = assemble(0, swaps)
    load.wait()
    answers(0)
    for level in range(1, levels):
        swaps = assemble(level, swaps)
    final = diag.at[levels]
    for i in range(1, n):
        start(
            remote(
                final,
                diag_got.at[me],
                diag_send.at[i],
                diag_recv.at[i],
                owner=lax.rem(me + i, n),
            )
        )
    diag_got[me] = diag[levels]

    for i in range(1, chips):
        answers(i)

    for level in range(levels):
        for i in range(1, chips):
            o = 2 * chip_from(i) + core
            here = blocks.at[level, span(o, depth)]
            remote(
                here, here, block_send.at[level, i], block_recv.at[level, i], owner=o
            ).wait_recv()
            start(
                remote(here, here, twin_send.at[level, i], twin_recv.at[level, i], owner=twin)
            )

    for i in range(1, n):
        o = lax.rem(me + n - i, n)
        here = diag_got.at[o]
        remote(here, here, diag_send.at[i], diag_recv.at[i], owner=o).wait_recv()
    share = LANES // depth
    for b in range(width // LANES):
        total = diag_got[b * share]
        for o in range(b * share + 1, (b + 1) * share):
            total = total + diag_got[o]
        scale[:, b * LANES : (b + 1) * LANES] = total

    for i in range(chips):
        c = chip_to(i)
        for k in range(2):
            if i == 0 and k == 0:
                continue
            at = 2 * i + k
            o = 2 * c + lax.rem(core + k, 2)
            here = back.at[span(o, cap)]
            remote(here, here, back_send.at[at], back_recv.at[at], owner=o).wait_recv()
        slot = lax.broadcasted_iota(I32, (own_rows, pair), 1) + c * pair
        route = one_hot(slot.astype(F32) == target_col[...])
        part = jnp.dot(route, back[span(c, pair), :], preferred_element_type=F32)
        response[...] = part if i == 0 else response[...] + part

    panel[0] = (response[...] / scale[:1, :]).astype(BF16)
    for level in range(levels):
        for i in range(chips):
            o = 2 * chip_from(i) + 1 - core
            here = blocks.at[level, span(o, depth)]
            remote(
                here, here, twin_send.at[level, i], twin_recv.at[level, i], owner=twin
            ).wait_recv()

        @pl.loop(0, width // 256)
        def _(t):
            tile = span(t, 256)
            coupled = lax.dot_general(
                panel[level],
                blocks[level, tile, :],
                (((1,), (1,)), ((), ())),
                preferred_element_type=F32,
            )
            value = (response[:, tile] - coupled) / scale[level + 1 : level + 2, tile]
            if level + 1 < levels:
                panel[level + 1, :, tile] = value.astype(BF16)
            else:
                out_ref[:, tile] = value

    for copy in started:
        copy.wait_send()


def body(
    port_rows,
    defect_owner,
    defect_half,
    defect_port,
    subcircuit_maps,
    schur_off,
    schur_diag,
    pivot_order,
):
    own_rows, width = port_rows.shape
    n = lax.axis_size("owner")
    levels = lax.axis_size("group").bit_length() - 1
    cap = 2 * own_rows // n
    depth = schur_off.shape[0]
    chips = n // 2
    assert subcircuit_maps.shape[0] == 2 and levels < 8 and LANES % depth == 0
    diag = schur_diag.reshape(1, depth)
    if depth < LANES:
        share = LANES // depth
        place = lax.rem(lax.axis_index("owner"), share)
        diag = jnp.where(jnp.arange(share)[:, None] == place, diag, 0.0).reshape(1, LANES)
    diag = jnp.broadcast_to(diag, (8, LANES))
    vmem = pl.BlockSpec(memory_space=pltpu.VMEM)
    dma = pltpu.SemaphoreType.DMA
    macs = own_rows * width * width * (4 + 1 + 1 + levels)
    return pl.pallas_call(
        functools.partial(kernel, n, levels, cap),
        out_shape=jax.ShapeDtypeStruct((own_rows, width), F32),
        in_specs=[vmem] * 4 + [pl.BlockSpec(memory_space=pl.ANY)] + [vmem] * 3,
        out_specs=vmem,
        scratch_shapes=[
            pltpu.VMEM(subcircuit_maps.shape, BF16),
            pltpu.VMEM((own_rows, width), BF16),
            pltpu.VMEM((n * cap, width), BF16),
            pltpu.VMEM((n * cap, width), BF16),
            pltpu.VMEM((n * cap, width), BF16),
            pltpu.VMEM((n * cap, width), BF16),
            pltpu.VMEM((n, 8, LANES), F32),
            pltpu.VMEM((n, 8, LANES), F32),
            pltpu.VMEM((levels, width, width), BF16),
            pltpu.VMEM((depth, width), F32),
            pltpu.VMEM((levels, depth, width), BF16),
            pltpu.VMEM((levels + 1, 8, LANES), F32),
            pltpu.VMEM((levels, 8, LANES), F32),
            pltpu.VMEM((n, 8, LANES), F32),
            pltpu.VMEM((8, width), F32),
            pltpu.VMEM((own_rows, 1), F32),
            pltpu.VMEM((own_rows, width), F32),
            pltpu.VMEM((levels, own_rows, width), BF16),
            dma,
            dma((n,)),
            dma((n,)),
            dma((n,)),
            dma((n,)),
            dma((n,)),
            dma((n,)),
            dma((levels,)),
            dma((levels,)),
            dma((levels,)),
            dma((levels,)),
            dma((levels, chips)),
            dma((levels, chips)),
            dma((levels, chips)),
            dma((levels, chips)),
            dma((n,)),
            dma((n,)),
        ],
        compiler_params=pltpu.CompilerParams(
            collective_id=0, has_side_effects=True, vmem_limit_bytes=56 * 1024 * 1024
        ),
        cost_estimate=pl.CostEstimate(
            flops=2 * macs, bytes_accessed=8 * own_rows * width * 2, transcendentals=0
        ),
    )(
        port_rows,
        defect_owner.reshape(1, own_rows),
        defect_half.reshape(1, own_rows),
        defect_port.reshape(1, own_rows),
        subcircuit_maps,
        schur_off,
        diag,
        pivot_order,
    )


def solution(mesh):
    return jax.shard_map(
        body,
        mesh=mesh,
        in_specs=(
            P(("group", "owner"), None),
            P(("group", "owner"), None),
            P(("group", "owner")),
            P(("group", "owner")),
            P(("group", "owner"), None, None),
            P(("group", "owner"), None),
            P(("group", "owner")),
            P(),
        ),
        out_specs=P(("group", "owner"), None),
        check_vma=False,
    )
```

time: 189 us -> 87.6 us (0.46)
  Pallas kernels: 0 us -> 83 us
  blocking collectives: 70.6 us -> 0 us
  waiting for transfers between devices: 41.1 us -> 0 us
  starting transfers between devices: 25 us -> 0 us
  matrix products: 24.2 us -> 0 us
  between operations: 13.6 us -> 0.01 us
  other arithmetic: 4.76 us -> 0 us
  local copies, waits for them, and re-layouts: 8.72 us -> 4.41 us
    pallas_call x0 -> x1, Pallas kernels: none -> 83 us  [body(): pl.pallas_call(functools.partial(kernel, n, levels, cap), out_shape=jax.S...]
    all_gather x3 -> x0, blocking collectives: 70.6 us -> none  [the longest x1 53.7 us: body(): first_diag = lax.all_gather(schur_diag, 'owner', axis=0, tiled=True)]
    all_to_all x2 -> x0, waiting for transfers between devices: 34.4 us -> none  [the longest x1 34.4 us: body(): lax.all_to_all(outgoing, 'owner', split_axis=0, concat_axis=0, tiled=True)]
    dot_general x4 -> x0, matrix products: 24.2 us -> none  [the longest x1 7.96 us: body(): jnp.einsum('oskp,spq->oskq', lax.all_to_all(outgoing, 'owner', split_axis...]
    all_to_all x2 -> x0, starting transfers between devices: 14.3 us -> none  [the longest x1 8.95 us: body(): lax.all_to_all(answer, 'owner', split_axis=0, concat_axis=0, tiled=True)]
    ppermute x4 -> x0, starting transfers between devices: 10.7 us -> none  [swapped(): lax.ppermute(shard, axis, [(i, i ^ 1 << stride) for i in range(lax.axis_s...]
    ppermute x4 -> x0, waiting for transfers between devices: 6.66 us -> none  [swapped(): lax.ppermute(shard, axis, [(i, i ^ 1 << stride) for i in range(lax.axis_s...]
    gather x2 -> x0, local copies, waits for them, and re-layouts: 5.63 us -> none  [body(): off_rows = off_rows + jnp.take(sibling_off, pivot_order[level], axis=1)]
  transfers between devices with their start and end apart: 8 -> 0, of which waited for: 2 -> 0; matrix products, arithmetic and copies ran while one was open for 12% -> 0% of each run, Pallas kernels for 0% -> 0%
where the time goes in v1:
time: 87.6 us; the launch traced here: 87.4 us
  Pallas kernels  83 us (95%)
  local copies, waits for them, and re-layouts  4.41 us (5%)
    pallas_call x1, Pallas kernels, body(): pl.pallas_call(functools.partial(kernel, n, levels, cap), out_shape=jax.S...  83 us
    unnamed x1, local copies, waits for them, and re-layouts  3.16 us

profile of v1, /device:TPU:1, one launch (start us, length us, event | category | flops | bytes accessed | tf_op | source)
XLA Modules:
  0.0 87.4 jit_solution(17903896864848767413)
XLA Ops:
  0.0 1.2 %broadcast_in_dim.2.diag_ref = f32[8,128]{1,0:T(8,128)} broadcast(f32[128]{0:T(128)} %param.14), dimensions={1} | broadcast | bytes 4608 | tf_op jit(solution)/shard_map/broadcast_in_dim | solution.py:378
  1.2 83.0 %shard_map.82 = f32[512,1024]{1,0:T(8,128)} custom-call(bf16[512,1024]{1,0:T(8,128)(2,1)} %rows_ref.1, s32[1,512]{1,0:T(1,128)} %bitcast.3, s32[1,512]{1,0:T(1,128)} %bitcast.4, s32[1,512]{1,0:T(1,128)} %bitcast.5, bf16[2,1024,1024]{2,1,0:T(8,128)(2,1)} %maps_ref.1, bf16[128,1024]{1,0:T(8,128)(2,1)} %off_ref.1, f32[8,128]{1,0:T(8,128)} %broadcast_in_dim.2.diag_ref, ...), custom_call_target="tpu_custom_call" | custom-call | flops 8589934592 | bytes 8388608 | tf_op jit(solution)/shard_map/pallas_call | solution.py:382
  84.2 3.2 %copy.10 = f32[512,1024]{1,0:T(8,128)} copy(f32[512,1024]{1,0:T(8,128)} %shard_map.82) | data formatting | bytes 4194304

commit v2 on v1

--- a/solution.py
+++ b/solution.py
@@ -30,7 +30,10 @@
     off_ref,
     diag_ref,
     order_ref,
-    out_ref,
+    panel_out,
+    response_out,
+    block_out,
+    scale_out,
     maps,
     stim,
     sent,
@@ -48,8 +51,12 @@
     scale,
     target_col,
     response,
+    rounded,
     panel,
+    pick,
+    across,
     map_sem,
+    out_sem,
     sent_send,
     sent_recv,
     meta_send,
@@ -66,6 +73,8 @@
     twin_recv,
     diag_send,
     diag_recv,
+    across_send,
+    across_recv,
 ):
     own_rows, width = rows_ref.shape
     depth = off_ref.shape[0]
@@ -75,6 +84,7 @@
     group = lax.axis_index("group")
     chip, core = lax.div(me, 2), lax.rem(me, 2)
     twin = chip * 2 + 1 - core
+    last = levels - 1
     started = []
 
     def partner(level):
@@ -128,20 +138,6 @@
     target_col[...] = jnp.sum(
         jnp.where(at_row == at_col, target_row, 0.0), axis=1, keepdims=True
     )
-    port_col = jnp.sum(
-        jnp.where(at_row == at_col, port_ref[...].astype(F32), 0.0), axis=1, keepdims=True
-    )
-    response[:, :LANES] = jnp.broadcast_to(port_col, (own_rows, LANES))
-
-    @pl.loop(0, own_rows // LANES)
-    def _(t):
-        tile = span(t, LANES)
-        column = lax.broadcasted_iota(I32, (LANES, width), 1).astype(F32)
-        injected = jnp.where(column == response[tile, :1], 8.0, 0.0)
-        stim[tile, :] = (rows_ref[tile, :].astype(F32) + injected).astype(BF16)
-
-    pl.semaphore_wait(barrier, n - 1 + levels)
-
     def start_swap(level):
         src = off_ref if level == 0 else blocks.at[level - 1, span(me, depth)]
         copy = remote(
@@ -158,8 +154,21 @@
         start(small)
         return copy, small
 
-    diag[0] = diag_ref[...]
+    diag[0] = jnp.broadcast_to(diag_ref[...], diag.shape[1:])
+    pl.semaphore_wait(barrier, n - 1 + levels)
     swaps = start_swap(0)
+
+    port_col = jnp.sum(
+        jnp.where(at_row == at_col, port_ref[...].astype(F32), 0.0), axis=1, keepdims=True
+    )
+    response[:, :LANES] = jnp.broadcast_to(port_col, (own_rows, LANES))
+
+    @pl.loop(0, own_rows // LANES)
+    def _(t):
+        tile = span(t, LANES)
+        column = lax.broadcasted_iota(I32, (LANES, width), 1).astype(F32)
+        injected = jnp.where(column == response[tile, :1], 8.0, 0.0)
+        stim[tile, :] = (rows_ref[tile, :].astype(F32) + injected).astype(BF16)
 
     for i in [*range(1, chips), 0]:
         c = chip_to(i)
@@ -202,9 +211,11 @@
         def _(t):
             tile = span(t, 256)
             order = order_ref[level : level + 1, tile]
-            pick = one_hot(lax.broadcasted_iota(I32, (width, 256), 0) == order)
+            chosen = one_hot(lax.broadcasted_iota(I32, (width, 256), 0) == order)
+            if level == last:
+                pick[:, tile] = chosen
             total = current[:depth, tile] + jnp.dot(
-                swap[level], pick, preferred_element_type=F32
+                swap[level], chosen, preferred_element_type=F32
             )
             current[:depth, tile] = total
             blocks[level, span(me, depth), tile] = total.astype(BF16)
@@ -215,7 +226,7 @@
         diag[level + 1] = jnp.where(at == level + 1, total, held)
         nxt = start_swap(level + 1) if level + 1 < levels else ()
         own = blocks.at[level, span(me, depth)]
-        for i in range(1, chips):
+        for i in range(1, chips if level < last else 1):
             start(
                 remote(
                     own,
@@ -268,11 +279,34 @@
                 )
             )
 
-    swaps = assemble(0, swaps)
-    load.wait()
-    answers(0)
-    for level in range(1, levels):
+    def collect(level):
+        for i in range(1, chips):
+            o = 2 * chip_from(i) + core
+            here = blocks.at[level, span(o, depth)]
+            remote(
+                here, here, block_send.at[level, i], block_recv.at[level, i], owner=o
+            ).wait_recv()
+            if level == last - 1:
+                start(
+                    remote(
+                        here,
+                        across.at[pl.ds(i * depth, depth)],
+                        across_send.at[i],
+                        across_recv.at[i],
+                        group=partner(last),
+                    )
+                )
+            start(
+                remote(here, here, twin_send.at[level, i], twin_recv.at[level, i], owner=twin)
+            )
+
+    for level in range(last):
         swaps = assemble(level, swaps)
+        if level == 0:
+            load.wait()
+            answers(0)
+        collect(level)
+    assemble(last, swaps)
     final = diag.at[levels]
     for i in range(1, n):
         start(
@@ -289,16 +323,24 @@
     for i in range(1, chips):
         answers(i)
 
-    for level in range(levels):
+    for i in range(1, chips):
+        here = across.at[pl.ds(i * depth, depth)]
+        remote(
+            here, here, across_send.at[i], across_recv.at[i], group=partner(last)
+        ).wait_recv()
+
+    @pl.loop(0, width // 256)
+    def _(t):
+        tile = span(t, 256)
+        permuted = jnp.dot(across[depth:, :], pick[:, tile], preferred_element_type=F32)
         for i in range(1, chips):
-            o = 2 * chip_from(i) + core
-            here = blocks.at[level, span(o, depth)]
-            remote(
-                here, here, block_send.at[level, i], block_recv.at[level, i], owner=o
-            ).wait_recv()
-            start(
-                remote(here, here, twin_send.at[level, i], twin_recv.at[level, i], owner=twin)
-            )
+            own = span(2 * chip_from(i) + core, depth)
+            part = permuted[(i - 1) * depth : i * depth]
+            blocks[last, own, tile] = (blocks[last - 1, own, tile].astype(F32) + part).astype(BF16)
+
+    for i in range(1, chips):
+        here = blocks.at[last, span(2 * chip_from(i) + core, depth)]
+        start(remote(here, here, twin_send.at[last, i], twin_recv.at[last, i], owner=twin))
 
     for i in range(1, n):
         o = lax.rem(me + n - i, n)
@@ -310,6 +352,17 @@
         for o in range(b * share + 1, (b + 1) * share):
             total = total + diag_got[o]
         scale[:, b * LANES : (b + 1) * LANES] = total
+
+    scale_out[...] = scale[...]
+    for level in range(levels):
+        for i in range(chips):
+            o = 2 * chip_from(i) + 1 - core
+            here = blocks.at[level, span(o, depth)]
+            remote(
+                here, here, twin_send.at[level, i], twin_recv.at[level, i], owner=twin
+            ).wait_recv()
+    stores = [pltpu.make_async_copy(blocks.at[last], block_out, out_sem.at[0])]
+    stores[0].start()
 
     for i in range(chips):
         c = chip_to(i)
@@ -325,14 +378,11 @@
         part = jnp.dot(route, back[span(c, pair), :], preferred_element_type=F32)
         response[...] = part if i == 0 else response[...] + part
 
+    rounded[...] = response[...].astype(BF16)
+    stores.append(pltpu.make_async_copy(rounded, response_out, out_sem.at[1]))
+    stores[1].start()
     panel[0] = (response[...] / scale[:1, :]).astype(BF16)
-    for level in range(levels):
-        for i in range(chips):
-            o = 2 * chip_from(i) + 1 - core
-            here = blocks.at[level, span(o, depth)]
-            remote(
-                here, here, twin_send.at[level, i], twin_recv.at[level, i], owner=twin
-            ).wait_recv()
+    for level in range(last):
 
         @pl.loop(0, width // 256)
         def _(t):
@@ -344,11 +394,12 @@
                 preferred_element_type=F32,
             )
             value = (response[:, tile] - coupled) / scale[level + 1 : level + 2, tile]
-            if level + 1 < levels:
-                panel[level + 1, :, tile] = value.astype(BF16)
-            else:
-                out_ref[:, tile] = value
-
+            panel[level + 1, :, tile] = value.astype(BF16)
+
+    stores.append(pltpu.make_async_copy(panel.at[last], panel_out, out_sem.at[2]))
+    stores[2].start()
+    for copy in stores:
+        copy.wait()
     for copy in started:
         copy.wait_send()
 
@@ -375,15 +426,20 @@
         share = LANES // depth
         place = lax.rem(lax.axis_index("owner"), share)
         diag = jnp.where(jnp.arange(share)[:, None] == place, diag, 0.0).reshape(1, LANES)
-    diag = jnp.broadcast_to(diag, (8, LANES))
     vmem = pl.BlockSpec(memory_space=pltpu.VMEM)
     dma = pltpu.SemaphoreType.DMA
     macs = own_rows * width * width * (4 + 1 + 1 + levels)
-    return pl.pallas_call(
+    hbm = pl.BlockSpec(memory_space=pl.ANY)
+    panel, response, block, scale = pl.pallas_call(
         functools.partial(kernel, n, levels, cap),
-        out_shape=jax.ShapeDtypeStruct((own_rows, width), F32),
-        in_specs=[vmem] * 4 + [pl.BlockSpec(memory_space=pl.ANY)] + [vmem] * 3,
-        out_specs=vmem,
+        out_shape=[
+            jax.ShapeDtypeStruct((own_rows, width), BF16),
+            jax.ShapeDtypeStruct((own_rows, width), BF16),
+            jax.ShapeDtypeStruct((width, width), BF16),
+            jax.ShapeDtypeStruct((8, width), F32),
+        ],
+        in_specs=[vmem] * 4 + [hbm] + [vmem] * 3,
+        out_specs=[hbm, hbm, hbm, vmem],
         scratch_shapes=[
             pltpu.VMEM(subcircuit_maps.shape, BF16),
             pltpu.VMEM((own_rows, width), BF16),
@@ -402,8 +458,12 @@
             pltpu.VMEM((8, width), F32),
             pltpu.VMEM((own_rows, 1), F32),
             pltpu.VMEM((own_rows, width), F32),
+            pltpu.VMEM((own_rows, width), BF16),
             pltpu.VMEM((levels, own_rows, width), BF16),
+            pltpu.VMEM((width, width), BF16),
+            pltpu.VMEM((chips * depth, width), BF16),
             dma,
+            dma((3,)),
             dma((n,)),
             dma((n,)),
             dma((n,)),
@@ -420,6 +480,8 @@
             dma((levels, chips)),
             dma((n,)),
             dma((n,)),
+            dma((chips,)),
+            dma((chips,)),
         ],
         compiler_params=pltpu.CompilerParams(
             collective_id=0, has_side_effects=True, vmem_limit_bytes=56 * 1024 * 1024
@@ -437,6 +499,10 @@
         diag,
         pivot_order,
     )
+    coupled = lax.dot_general(
+        panel, block, (((1,), (1,)), ((), ())), preferred_element_type=F32
+    )
+    return (response.astype(F32) - coupled) / scale[levels][None, :]
 
 
 def solution(mesh):

time: 87.6 us -> 88.4 us (level)
  matrix products: 0 us -> 4.78 us
  local copies, waits for them, and re-layouts: 4.41 us -> 0.76 us
    dot_general x0 -> x1, matrix products: none -> 4.78 us  [body(): lax.dot_general(panel, block, (((1,), (1,)), ((), ())), preferred_element...]
    unnamed x1 -> x0, local copies, waits for them, and re-layouts: 3.16 us -> none
    broadcast_in_dim x1 -> x0, local copies, waits for them, and re-layouts: 1.25 us -> none  [body(): diag = jnp.broadcast_to(diag, (8, LANES))]
where the time goes in v2:
time: 88.4 us; the launch traced here: 88.2 us
  Pallas kernels  82.6 us (93%)
  matrix products  4.78 us (5%)
    pallas_call x1, Pallas kernels, body(): pl.pallas_call(functools.partial(kernel, n, levels, cap), out_shape=[jax....  82.6 us
    dot_general x1, matrix products, body(): lax.dot_general(panel, block, (((1,), (1,)), ((), ())), preferred_element...  4.78 us

profile of v2, /device:TPU:1, one launch (start us, length us, event | category | flops | bytes accessed | tf_op | source)
XLA Modules:
  0.0 88.2 jit_solution(13835711887145844139)
XLA Ops:
  0.0 82.6 %shard_map.82 = (bf16[512,1024]{1,0:T(8,128)(2,1)}, bf16[512,1024]{1,0:T(8,128)(2,1)}, bf16[1024,1024]{1,0:T(8,128)(2,1)}, f32[8,1024]{1,0:T(8,128)}) custom-call(bf16[512,1024]{1,0:T(8,128)(2,1)} %rows_ref.1, s32[1,512]{1,0:T(1,128)} %bitcast.8, s32[1,512]{1,0:T(1,128)} %bitcast.9, s32[1,512]{1,0:T(1,128)} %bitcast.10, bf16[2,1024,1024]{2,1,0:T(8,128)(2,1)} %maps_ref.1, ...), custom_call_target="tpu_custom_call" | custom-call | flops 8589934592 | bytes 8388608 | tf_op jit(solution)/shard_map/pallas_call | solution.py:433
  82.6 0.8 slice.3
  83.4 4.8 %subtract_divide_fusion = f32[512,1024]{1,0:T(8,128)} fusion(bf16[512,1024]{1,0:T(8,128)(2,1)} %get-tuple-element.9, bf16[512,1024]{1,0:T(8,128)(2,1)} %get-tuple-element.10, bf16[1024,1024]{1,0:T(8,128)(2,1)} %get-tuple-element.11, f32[1024]{0:T(1024)S(1)} %bitcast.7), kind=kOutput, calls=%fused_computation | convolution fusion | flops 1075314688 | bytes 6295552 | tf_op jit(solution)/shard_map/dot_general | solution.py:502

commit v3 on v2

--- a/solution.py
+++ b/solution.py
@@ -85,6 +85,8 @@
     chip, core = lax.div(me, 2), lax.rem(me, 2)
     twin = chip * 2 + 1 - core
     last = levels - 1
+    far = chips - 1
+    served = range(chips - 1, 0, -1)
     started = []
 
     def partner(level):
@@ -108,11 +110,12 @@
     def span(at, size):
         return pl.ds(pl.multiple_of(at * size, size), size)
 
-    def chip_to(i):
-        return lax.rem(chip + i, chips)
-
-    def chip_from(i):
-        return lax.rem(chip + chips - i, chips)
+    def chip_at(i):
+        other = chip
+        for bit in range(chips.bit_length() - 1):
+            if i >> bit & 1:
+                other = other + (1 << bit) * (1 - 2 * lax.rem(lax.div(chip, 1 << bit), 2))
+        return other
 
     barrier = pltpu.get_barrier_semaphore()
     for i in range(1, n):
@@ -170,8 +173,8 @@
         injected = jnp.where(column == response[tile, :1], 8.0, 0.0)
         stim[tile, :] = (rows_ref[tile, :].astype(F32) + injected).astype(BF16)
 
-    for i in [*range(1, chips), 0]:
-        c = chip_to(i)
+    for i in [*served, 0]:
+        c = chip_at(i)
         slot = lax.broadcasted_iota(I32, (pair, own_rows), 0) + c * pair
         route = one_hot(slot.astype(F32) == target_row)
         sent[span(c, pair), :] = jnp.dot(
@@ -226,21 +229,21 @@
         diag[level + 1] = jnp.where(at == level + 1, total, held)
         nxt = start_swap(level + 1) if level + 1 < levels else ()
         own = blocks.at[level, span(me, depth)]
-        for i in range(1, chips if level < last else 1):
+        for i in range(1, chips if level < last else far):
             start(
                 remote(
                     own,
                     own,
                     block_send.at[level, i],
                     block_recv.at[level, i],
-                    owner=2 * chip_to(i) + core,
+                    owner=2 * chip_at(i) + core,
                 )
             )
         start(remote(own, own, twin_send.at[level, 0], twin_recv.at[level, 0], owner=twin))
         return nxt
 
     def answers(i):
-        c = chip_from(i)
+        c = chip_at(i)
         for k in range(2):
             if i == 0 and k == 0:
                 continue
@@ -280,22 +283,14 @@
             )
 
     def collect(level):
-        for i in range(1, chips):
-            o = 2 * chip_from(i) + core
+        for i in range(1, chips if level < last else far):
+            o = 2 * chip_at(i) + core
             here = blocks.at[level, span(o, depth)]
             remote(
                 here, here, block_send.at[level, i], block_recv.at[level, i], owner=o
             ).wait_recv()
-            if level == last - 1:
-                start(
-                    remote(
-                        here,
-                        across.at[pl.ds(i * depth, depth)],
-                        across_send.at[i],
-                        across_recv.at[i],
-                        group=partner(last),
-                    )
-                )
+            if level == last - 1 and i == far:
+                start(remote(here, across, across_send, across_recv, group=partner(last)))
             start(
                 remote(here, here, twin_send.at[level, i], twin_recv.at[level, i], owner=twin)
             )
@@ -305,8 +300,9 @@
         if level == 0:
             load.wait()
             answers(0)
+    assemble(last, swaps)
+    for level in range(last):
         collect(level)
-    assemble(last, swaps)
     final = diag.at[levels]
     for i in range(1, n):
         start(
@@ -320,27 +316,24 @@
         )
     diag_got[me] = diag[levels]
 
-    for i in range(1, chips):
+    for i in served:
         answers(i)
 
-    for i in range(1, chips):
-        here = across.at[pl.ds(i * depth, depth)]
-        remote(
-            here, here, across_send.at[i], across_recv.at[i], group=partner(last)
-        ).wait_recv()
+    collect(last)
+
+    remote(across, across, across_send, across_recv, group=partner(last)).wait_recv()
+    theirs = span(2 * chip_at(far) + core, depth)
 
     @pl.loop(0, width // 256)
     def _(t):
         tile = span(t, 256)
-        permuted = jnp.dot(across[depth:, :], pick[:, tile], preferred_element_type=F32)
-        for i in range(1, chips):
-            own = span(2 * chip_from(i) + core, depth)
-            part = permuted[(i - 1) * depth : i * depth]
-            blocks[last, own, tile] = (blocks[last - 1, own, tile].astype(F32) + part).astype(BF16)
-
-    for i in range(1, chips):
-        here = blocks.at[last, span(2 * chip_from(i) + core, depth)]
-        start(remote(here, here, twin_send.at[last, i], twin_recv.at[last, i], owner=twin))
+        permuted = jnp.dot(across[...], pick[:, tile], preferred_element_type=F32)
+        blocks[last, theirs, tile] = (
+            blocks[last - 1, theirs, tile].astype(F32) + permuted
+        ).astype(BF16)
+
+    here = blocks.at[last, theirs]
+    start(remote(here, here, twin_send.at[last, far], twin_recv.at[last, far], owner=twin))
 
     for i in range(1, n):
         o = lax.rem(me + n - i, n)
@@ -353,10 +346,10 @@
             total = total + diag_got[o]
         scale[:, b * LANES : (b + 1) * LANES] = total
 
-    scale_out[...] = scale[...]
+    scale_out[...] = scale[levels : levels + 1, :]
     for level in range(levels):
         for i in range(chips):
-            o = 2 * chip_from(i) + 1 - core
+            o = 2 * chip_at(i) + 1 - core
             here = blocks.at[level, span(o, depth)]
             remote(
                 here, here, twin_send.at[level, i], twin_recv.at[level, i], owner=twin
@@ -364,8 +357,8 @@
     stores = [pltpu.make_async_copy(blocks.at[last], block_out, out_sem.at[0])]
     stores[0].start()
 
-    for i in range(chips):
-        c = chip_to(i)
+    for i in [0, *served]:
+        c = chip_at(i)
         for k in range(2):
             if i == 0 and k == 0:
                 continue
@@ -420,7 +413,7 @@
     cap = 2 * own_rows // n
     depth = schur_off.shape[0]
     chips = n // 2
-    assert subcircuit_maps.shape[0] == 2 and levels < 8 and LANES % depth == 0
+    assert subcircuit_maps.shape[0] == 2 and 1 < levels < 8 and chips & (chips - 1) == 0 and LANES % depth == 0
     diag = schur_diag.reshape(1, depth)
     if depth < LANES:
         share = LANES // depth
@@ -436,7 +429,7 @@
             jax.ShapeDtypeStruct((own_rows, width), BF16),
             jax.ShapeDtypeStruct((own_rows, width), BF16),
             jax.ShapeDtypeStruct((width, width), BF16),
-            jax.ShapeDtypeStruct((8, width), F32),
+            jax.ShapeDtypeStruct((1, width), F32),
         ],
         in_specs=[vmem] * 4 + [hbm] + [vmem] * 3,
         out_specs=[hbm, hbm, hbm, vmem],
@@ -461,7 +454,7 @@
             pltpu.VMEM((own_rows, width), BF16),
             pltpu.VMEM((levels, own_rows, width), BF16),
             pltpu.VMEM((width, width), BF16),
-            pltpu.VMEM((chips * depth, width), BF16),
+            pltpu.VMEM((depth, width), BF16),
             dma,
             dma((3,)),
             dma((n,)),
@@ -480,8 +473,8 @@
             dma((levels, chips)),
             dma((n,)),
             dma((n,)),
-            dma((chips,)),
-            dma((chips,)),
+            dma,
+            dma,
         ],
         compiler_params=pltpu.CompilerParams(
             collective_id=0, has_side_effects=True, vmem_limit_bytes=56 * 1024 * 1024
@@ -502,7 +495,7 @@
     coupled = lax.dot_general(
         panel, block, (((1,), (1,)), ((), ())), preferred_element_type=F32
     )
-    return (response.astype(F32) - coupled) / scale[levels][None, :]
+    return (response.astype(F32) - coupled) / scale
 
 
 def solution(mesh):

time: 88.4 us -> 81.2 us (0.919)
  Pallas kernels: 82.6 us -> 76.2 us
    pallas_call x1, Pallas kernels: 82.6 us -> 76.2 us  [body(): pl.pallas_call(functools.partial(kernel, n, levels, cap), out_shape=[jax....]
where the time goes in v3:
time: 81.2 us; the launch traced here: 81 us
  Pallas kernels  76.2 us (94%)
  matrix products  4.79 us (6%)
    pallas_call x1, Pallas kernels, body(): pl.pallas_call(functools.partial(kernel, n, levels, cap), out_shape=[jax....  76.2 us
    dot_general x1, matrix products, body(): lax.dot_general(panel, block, (((1,), (1,)), ((), ())), preferred_element...  4.79 us

profile of v3, /device:TPU:1, one launch (start us, length us, event | category | flops | bytes accessed | tf_op | source)
XLA Modules:
  0.0 81.0 jit_solution(14098844918350660840)
XLA Ops:
  0.0 76.2 %shard_map.82 = (bf16[512,1024]{1,0:T(8,128)(2,1)}, bf16[512,1024]{1,0:T(8,128)(2,1)}, bf16[1024,1024]{1,0:T(8,128)(2,1)}, f32[1,1024]{1,0:T(1,128)}) custom-call(bf16[512,1024]{1,0:T(8,128)(2,1)} %rows_ref.1, s32[1,512]{1,0:T(1,128)} %bitcast.7, s32[1,512]{1,0:T(1,128)} %bitcast.8, s32[1,512]{1,0:T(1,128)} %bitcast.9, bf16[2,1024,1024]{2,1,0:T(8,128)(2,1)} %maps_ref.1, ...), custom_call_target="tpu_custom_call" | custom-call | flops 8589934592 | bytes 8388608 | tf_op jit(solution)/shard_map/pallas_call | solution.py:426
  76.2 4.8 %subtract_divide_fusion = f32[512,1024]{1,0:T(8,128)} fusion(bf16[512,1024]{1,0:T(8,128)(2,1)} %get-tuple-element.9, bf16[512,1024]{1,0:T(8,128)(2,1)} %get-tuple-element.10, bf16[1024,1024]{1,0:T(8,128)(2,1)} %get-tuple-element.11, f32[1024]{0:T(1024)} %bitcast.11), kind=kOutput, calls=%fused_computation | convolution fusion | flops 1075314688 | bytes 6295552 | tf_op jit(solution)/shard_map/dot_general | solution.py:495

commit v4 on v3

--- a/solution.py
+++ b/solution.py
@@ -204,6 +204,19 @@
                 )
             )
 
+    def spread(level, stop):
+        own = blocks.at[level, span(me, depth)]
+        for i in range(1, stop):
+            start(
+                remote(
+                    own,
+                    own,
+                    block_send.at[level, i],
+                    block_recv.at[level, i],
+                    owner=2 * chip_at(i) + core,
+                )
+            )
+
     def assemble(level, pending):
         for copy in pending:
             copy.wait_recv()
@@ -229,16 +242,8 @@
         diag[level + 1] = jnp.where(at == level + 1, total, held)
         nxt = start_swap(level + 1) if level + 1 < levels else ()
         own = blocks.at[level, span(me, depth)]
-        for i in range(1, chips if level < last else far):
-            start(
-                remote(
-                    own,
-                    own,
-                    block_send.at[level, i],
-                    block_recv.at[level, i],
-                    owner=2 * chip_at(i) + core,
-                )
-            )
+        if level < last:
+            spread(level, chips)
         start(remote(own, own, twin_send.at[level, 0], twin_recv.at[level, 0], owner=twin))
         return nxt
 
@@ -253,6 +258,8 @@
             remote(here, here, sent_send.at[at], sent_recv.at[at], owner=o).wait_recv()
             tag = meta_got.at[o]
             remote(tag, tag, meta_send.at[at], meta_recv.at[at], owner=o).wait_recv()
+        if i == far:
+            spread(last, far)
         at = lax.broadcasted_iota(I32, (pair, 1), 0)
         even, odd = meta_got[2 * c], meta_got[2 * c + 1]
         limit = jnp.where(at < cap, even[:1, :1], odd[:1, :1] + cap)

time: 81.2 us -> 82 us (level)
  Pallas kernels: 76.2 us -> 77.1 us
    pallas_call x1, Pallas kernels: 76.2 us -> 77.1 us  [body(): pl.pallas_call(functools.partial(kernel, n, levels, cap), out_shape=[jax....]
where the time goes in v4:
time: 82 us; the launch traced here: 81.9 us
  Pallas kernels  77.1 us (94%)
  matrix products  4.78 us (6%)
    pallas_call x1, Pallas kernels, body(): pl.pallas_call(functools.partial(kernel, n, levels, cap), out_shape=[jax....  77.1 us
    dot_general x1, matrix products, body(): lax.dot_general(panel, block, (((1,), (1,)), ((), ())), preferred_element...  4.78 us

profile of v4, /device:TPU:1, one launch (start us, length us, event | category | flops | bytes accessed | tf_op | source)
XLA Modules:
  0.0 81.9 jit_solution(516946918448380292)
XLA Ops:
  0.0 77.1 %shard_map.82 = (bf16[512,1024]{1,0:T(8,128)(2,1)}, bf16[512,1024]{1,0:T(8,128)(2,1)}, bf16[1024,1024]{1,0:T(8,128)(2,1)}, f32[1,1024]{1,0:T(1,128)}) custom-call(bf16[512,1024]{1,0:T(8,128)(2,1)} %rows_ref.1, s32[1,512]{1,0:T(1,128)} %bitcast.7, s32[1,512]{1,0:T(1,128)} %bitcast.8, s32[1,512]{1,0:T(1,128)} %bitcast.9, bf16[2,1024,1024]{2,1,0:T(8,128)(2,1)} %maps_ref.1, ...), custom_call_target="tpu_custom_call" | custom-call | flops 8589934592 | bytes 8388608 | tf_op jit(solution)/shard_map/pallas_call | solution.py:433
  77.1 4.8 %subtract_divide_fusion = f32[512,1024]{1,0:T(8,128)} fusion(bf16[512,1024]{1,0:T(8,128)(2,1)} %get-tuple-element.9, bf16[512,1024]{1,0:T(8,128)(2,1)} %get-tuple-element.10, bf16[1024,1024]{1,0:T(8,128)(2,1)} %get-tuple-element.11, f32[1024]{0:T(1024)} %bitcast.11), kind=kOutput, calls=%fused_computation | convolution fusion | flops 1075314688 | bytes 6295552 | tf_op jit(solution)/shard_map/dot_general | solution.py:502
